TPU v7x, 32 devices: a whole 2x2x4 slice. The times are simulated.
32 devices in a mesh: chan: 2 (over x), tm: 8 (over z, y), dp: 2 (over core).
Axes of the slice: x: 2, y: 2, z: 4, core: 2. Of those that a mesh axis runs over, the one named last changes fastest.
Arguments:
- contexts: bfloat16 [512, 4, 16384], P('tm', 'dp', 'chan'), may hold values from -6 to 6
- cotangent: bfloat16 [512, 4, 16384], P('tm', 'dp', 'chan'), may hold values from -6 to 6
- w_in: bfloat16 [16384, 8192], P('chan', 'tm'), may hold values from -0.046875 to 0.046875
- w_out: bfloat16 [8192, 16384], P('tm', 'chan'), may hold values from -0.0625 to 0.0625
- time_weight: bfloat16 [512, 512], replicated, may hold values from -0.25 to 0.25
Outputs:
- grad_contexts: bfloat16 [512, 4, 16384], P('tm', 'dp', 'chan')
- grad_w_in: float32 [16384, 8192], P('chan', ('tm', 'dp'))
- grad_w_out: float32 [8192, 16384], P(('tm', 'dp'), 'chan')
- grad_time: float32 [512, 512], replicated
All inputs are finite; a program needn't handle non-finite values.
Results may differ from a plain program's by a relative error of at most 0.0057.
Values may be sent and summed in bfloat16 or wider, within the bound.
A program may use at most 384 MiB of HBM per device.

v0:
```python
import math

import jax
import jax.numpy as jnp
from jax import lax
from jax.sharding import PartitionSpec as P

tanh_scale = math.sqrt(2.0 / math.pi)
cubic_term = 0.044715


def gelu_pair(value):
    inner = jnp.tanh(tanh_scale * (value + cubic_term * value * value * value))
    result = 0.5 * value * (1.0 + inner)
    slope = 0.5 * (1.0 + inner) + 0.5 * value * (1.0 - inner * inner) * tanh_scale * (
        1.0 + 3.0 * cubic_term * value * value
    )
    return (result, slope)


def hidden_finish(hidden_pre, hidden_grad):
    act_hidden, slope_hidden = gelu_pair(hidden_pre)
    return (act_hidden.astype(jnp.bfloat16), (hidden_grad * slope_hidden).astype(jnp.bfloat16))


def on_device(contexts, cotangent, w_in, w_out, time_weight):
    local_len, batch_dev, width_dev = contexts.shape
    whole_x, whole_dy = (
        lax.all_gather(contexts, "tm", axis=0, tiled=True),
        lax.all_gather(cotangent, "tm", axis=0, tiled=True),
    )
    length = whole_x.shape[0]
    flat_x = whole_x.reshape(length, batch_dev * width_dev)
    pre_time = jnp.dot(time_weight, flat_x, preferred_element_type=jnp.float32)
    act_time, slope_time = gelu_pair(pre_time)
    mixed = (
        (flat_x.astype(jnp.float32) + act_time)
        .astype(jnp.bfloat16)
        .reshape(length * batch_dev, width_dev)
    )
    grad_rows = whole_dy.reshape(length * batch_dev, width_dev)
    hidden_part = jnp.dot(mixed, w_in, preferred_element_type=jnp.float32)
    hgrad_part = jnp.einsum("rc,hc->rh", grad_rows, w_out, preferred_element_type=jnp.float32)
    hidden_pre, hidden_grad = lax.psum((hidden_part, hgrad_part), "chan")
    activation, pre_grad = hidden_finish(hidden_pre, hidden_grad)
    win_part = jnp.einsum("rc,rh->ch", mixed, pre_grad, preferred_element_type=jnp.float32)
    wout_part = jnp.einsum("rh,rc->hc", activation, grad_rows, preferred_element_type=jnp.float32)
    grad_w_in, grad_w_out = (
        lax.psum_scatter(win_part, "dp", scatter_dimension=1, tiled=True),
        lax.psum_scatter(wout_part, "dp", scatter_dimension=0, tiled=True),
    )
    position = lax.axis_index("tm")
    my_rows = local_len * batch_dev
    feature_sum = lax.psum_scatter(
        jnp.einsum("rh,ch->rc", pre_grad, w_in, preferred_element_type=jnp.float32),
        "tm",
        scatter_dimension=0,
        tiled=True,
    )
    own_dy = cotangent.reshape(my_rows, width_dev)
    mixed_grad = (own_dy.astype(jnp.float32) + feature_sum).reshape(
        local_len, batch_dev * width_dev
    )
    own_slope = lax.dynamic_slice_in_dim(slope_time, position * local_len, local_len, 0)
    own_gate = (mixed_grad * own_slope).astype(jnp.bfloat16)
    all_gate = lax.all_gather(own_gate, "tm", axis=0, tiled=True)
    own_columns = lax.dynamic_slice_in_dim(time_weight, position * local_len, local_len, 1)
    back = jnp.einsum("tl,tk->lk", own_columns, all_gate, preferred_element_type=jnp.float32)
    grad_contexts = (
        (mixed_grad + back).reshape(local_len, batch_dev, width_dev).astype(jnp.bfloat16)
    )
    time_part = jnp.einsum("tk,lk->tl", own_gate, flat_x, preferred_element_type=jnp.float32)
    time_rows = lax.psum(time_part, ("chan", "dp"))
    grad_time = lax.all_gather(time_rows, "tm", axis=0, tiled=True)
    return (grad_contexts, grad_w_in, grad_w_out, grad_time)


def solution(mesh):
    return jax.shard_map(
        on_device,
        mesh=mesh,
        in_specs=(
            P("tm", "dp", "chan"),
            P("tm", "dp", "chan"),
            P("chan", "tm"),
            P("tm", "chan"),
            P(),
        ),
        out_specs=(P("tm", "dp", "chan"), P("chan", ("tm", "dp")), P(("tm", "dp"), "chan"), P()),
        check_vma=False,
    )
```

profile of v0, /device:TPU:0, one launch (start us, length us, event | category | flops | bytes accessed | tf_op | source)
XLA Modules:
  0.0 1728.0 jit_solution(15502225100952589161)
XLA Ops:
  7.2 0.0 copy-start
  7.2 0.0 all-gather.7.cloned.1.call-start
  7.2 0.7 all-gather.7.cloned.1.call-update
  7.9 0.0 all-gather.5.cloned.1.call-start
  8.0 0.7 all-gather.5.cloned.1.call-update
  8.7 0.0 all-reduce.6.cloned.1.call-start
  8.7 231.8 %all-gather.7.cloned.1.call-done = bf16[512,2,8192]{2,1,0:T(2,128)(2,1)} async-done(((bf16[64,2,8192]{2,1,0:T(2,128)(2,1)}), bf16[512,2,8192]{2,1,0:T(2,128)(2,1)}) %all-gather.7.cloned.1.call-update) | async-done | bytes 16777232 | tf_op jit(solution)/shard_map/all_gather | solution.py:29
  240.5 18.7 %copy.9 = bf16[64,8,2,8192]{3,1,2,0:T(8,128)(2,1)} copy(bf16[64,8,2,8192]{3,2,1,0:T(2,128)(2,1)} %bitcast.18) | data formatting | bytes 33554432
  259.2 60.1 %fusion.1 = (f32[512,16384]{1,0:T(8,128)}, f32[512,16384]{1,0:T(8,128)}, bf16[512,16384]{1,0:T(8,128)(2,1)}, f32[512,16384]{1,0:T(8,128)}, f32[512,16384]{1,0:T(8,128)}) fusion(bf16[512,16384]{1,0:T(8,128)(2,1)} %bitcast.16, bf16[512,512]{1,0:T(8,128)(2,1)S(1)} %copy-done), kind=kOutput, calls=%fused_computation.2 | convolution fusion | flops 8682209280 | bytes 168296448 | tf_op jit(solution)/shard_map/dot_general | solution.py:34
  319.4 25.5 %reshape.27 = bf16[1024,8192]{1,0:T(8,128)(2,1)} reshape(bf16[512,16384]{1,0:T(8,128)(2,1)} %get-tuple-element.8) | data formatting | bytes 33554432 | tf_op jit(solution)/shard_map/reshape | solution.py:39
  344.8 23.5 %fusion.29 = f32[1024,1024]{1,0:T(8,128)} fusion(bf16[1024,8192]{1,0:T(8,128)(2,1)} %reshape.27, bf16[8192,1024]{1,0:T(8,128)(2,1)} %param.7), kind=kOutput, calls=%fused_computation.41 | convolution fusion | flops 17179869184 | bytes 37748736 | tf_op jit(solution)/shard_map/dot_general | solution.py:42
  368.3 100.1 %all-gather.5.cloned.1.call-done = bf16[512,2,8192]{2,1,0:T(2,128)(2,1)} async-done(((bf16[64,2,8192]{2,1,0:T(2,128)(2,1)}), bf16[512,2,8192]{2,1,0:T(2,128)(2,1)}) %all-gather.5.cloned.1.call-update) | async-done | bytes 16777232 | tf_op jit(solution)/shard_map/all_gather | solution.py:30
  468.4 24.8 %reshape.25 = bf16[1024,8192]{1,0:T(8,128)(2,1)} reshape(bf16[512,2,8192]{2,1,0:T(2,128)(2,1)} %all-gather.5.cloned.1.call-done) | data formatting | bytes 33554432 | tf_op jit(solution)/shard_map/reshape | solution.py:41
  493.2 23.7 %fusion.28 = f32[1024,1024]{1,0:T(8,128)} fusion(bf16[1024,8192]{1,0:T(8,128)(2,1)} %reshape.25, bf16[1024,8192]{1,0:T(8,128)(2,1)} %param.8), kind=kOutput, calls=%fused_computation.40 | convolution fusion | flops 17179869184 | bytes 37748736 | tf_op jit(solution)/shard_map/rc,hc->rh/dot_general | solution.py:43
  517.0 0.0 all-reduce.6.cloned.1.call-update
  517.0 0.2 reduce-scatter.4.cloned.1.call-start
  517.2 196.6 %all-reduce.6.cloned.1.call-done = (f32[1024,1024]{1,0:T(8,128)}, f32[1024,1024]{1,0:T(8,128)}) async-done(((f32[1024,1024]{1,0:T(8,128)}, f32[1024,1024]{1,0:T(8,128)}), (f32[1024,1024]{1,0:T(8,128)}, f32[1024,1024]{1,0:T(8,128)})) %all-reduce.6.cloned.1.call-update) | async-done | bytes 8388624 | tf_op jit(solution)/shard_map/psum | solution.py:44
  713.8 4.9 fusion.9
  718.8 1.3 copy-done.3
  720.1 25.2 %fusion.30 = f32[1024,8192]{1,0:T(8,128)} fusion(bf16[1024,1024]{1,0:T(8,128)(2,1)S(1)} %fusion.9, bf16[8192,1024]{1,0:T(8,128)(2,1)} %param.7), kind=kOutput, calls=%fused_computation.42 | convolution fusion | flops 17179869184 | bytes 52428800 | tf_op jit(solution)/shard_map/rh,ch->rc/dot_general | solution.py:55
  745.3 0.0 reduce-scatter.4.cloned.1.call-update
  745.3 0.0 all-reduce.4.cloned.1.call-start
  745.4 1.5 copy-done.2
  746.9 2.6 reshape.29
  749.5 539.7 %reduce-scatter.4.cloned.1.call-done = f32[128,8192]{1,0:T(8,128)} async-done(((f32[1024,8192]{1,0:T(8,128)}), f32[128,8192]{1,0:T(8,128)}) %reduce-scatter.4.cloned.1.call-update) | async-done | bytes 4194320 | tf_op jit(solution)/shard_map/reduce_scatter | solution.py:54
  1289.3 5.9 add.58
  1295.2 5.3 reshape.28
  1300.4 7.8 fusion.14
  1308.3 12.4 fusion.32
  1320.7 0.0 all-reduce.4.cloned.1.call-update
  1320.7 0.0 all-gather.11.cloned.1.call-start
  1320.8 30.6 %all-reduce.4.cloned.1.call-done = f32[64,512]{1,0:T(8,128)} async-done(((f32[64,512]{1,0:T(8,128)}), f32[64,512]{1,0:T(8,128)}) %all-reduce.4.cloned.1.call-update) | async-done | bytes 131088 | tf_op jit(solution)/shard_map/psum | solution.py:73
  1351.4 0.0 all-gather.11.cloned.1.call-update
  1351.4 0.0 all-gather.9.cloned.1.call-start
  1351.5 0.7 all-gather.9.cloned.1.call-update
  1352.2 0.3 reduce-scatter.6.cloned.1.call-start
  1352.4 27.8 %fusion.31 = f32[8192,1024]{1,0:T(8,128)} fusion(bf16[1024,8192]{1,0:T(8,128)(2,1)} %reshape.27, bf16[1024,1024]{1,0:T(8,128)(2,1)} %copy-done.3), kind=kOutput, calls=%fused_computation.43 | convolution fusion | flops 17179869184 | bytes 52428800 | tf_op jit(solution)/shard_map/rc,rh->ch/dot_general | solution.py:46
  1380.2 0.0 reduce-scatter.6.cloned.1.call-update
  1380.2 0.3 reduce-scatter.8.cloned.1.call-start
  1380.5 30.1 %fusion.17 = f32[1024,8192]{1,0:T(8,128)} fusion(bf16[1024,8192]{1,0:T(8,128)(2,1)} %reshape.25, f32[1024,1024]{1,0:T(8,128)} %get-tuple-element.5), kind=kOutput, calls=%fused_computation.29 | convolution fusion | flops 17189306368 | bytes 54525952 | tf_op jit(solution)/shard_map/rh,rc->hc/dot_general | solution.py:47
  1410.6 0.0 reduce-scatter.8.cloned.1.call-update
  1410.6 0.0 all-gather.11.cloned.1.call-done
  1410.6 212.4 %all-gather.9.cloned.1.call-done = bf16[512,16384]{1,0:T(8,128)(2,1)} async-done(((bf16[64,16384]{1,0:T(8,128)(2,1)}), bf16[512,16384]{1,0:T(8,128)(2,1)}) %all-gather.9.cloned.1.call-update) | async-done | bytes 16777232 | tf_op jit(solution)/shard_map/all_gather | solution.py:66
  1623.1 10.1 fusion.2
  1633.2 2.8 convert_element_type.34
  1636.0 33.4 %reduce-scatter.6.cloned.1.call-done = f32[8192,512]{1,0:T(8,128)} async-done(((f32[8192,1024]{1,0:T(8,128)}), f32[8192,512]{1,0:T(8,128)}) %reduce-scatter.6.cloned.1.call-update) | async-done | bytes 16777232 | tf_op jit(solution)/shard_map/reduce_scatter | solution.py:49
  1669.4 49.4 %reduce-scatter.8.cloned.1.call-done = f32[512,8192]{1,0:T(8,128)} async-done(((f32[1024,8192]{1,0:T(8,128)}), f32[512,8192]{1,0:T(8,128)}) %reduce-scatter.8.cloned.1.call-update) | async-done | bytes 16777232 | tf_op jit(solution)/shard_map/reduce_scatter | solution.py:50
  1718.8 2.3 copy.14
  (5 shorter events, 0.0 us)
Async XLA Ops:
  7.2 252.1 %copy-start = (bf16[512,512]{1,0:T(8,128)(2,1)S(1)}, bf16[512,512]{1,0:T(8,128)(2,1)}, u32[]{:S(2)}) copy-start(bf16[512,512]{1,0:T(8,128)(2,1)} %param.9) | copy-start | bytes 1572868
  7.2 233.3 %all-gather.7.cloned.1.call-start = ((), (), s32[]{:S(2)}) async-start(), calls=%async_computation.4 | async-start | bytes 18874368 | tf_op jit(solution)/shard_map/all_gather | solution.py:29
  7.9 460.5 %all-gather.5.cloned.1.call-start = ((), (), s32[]{:S(2)}) async-start(), calls=%async_computation.3 | async-start | bytes 18874368 | tf_op jit(solution)/shard_map/all_gather | solution.py:30
  8.7 705.2 %all-reduce.6.cloned.1.call-start = ((), (), s32[]{:S(2)}) async-start(), calls=%async_computation.11 | async-start | bytes 16777216 | tf_op jit(solution)/shard_map/psum | solution.py:44
  517.0 772.3 %reduce-scatter.4.cloned.1.call-start = ((), (), s32[]{:S(2)}) async-start(), calls=%async_computation.5 | async-start | bytes 37748736 | tf_op jit(solution)/shard_map/reduce_scatter | solution.py:54
  718.8 1.3 copy-start.3
  745.3 1.6 copy-start.2
  745.3 606.0 %all-reduce.4.cloned.1.call-start = ((), (), s32[]{:S(2)}) async-start(), calls=%async_computation.9 | async-start | bytes 262144 | tf_op jit(solution)/shard_map/psum | solution.py:73
  1308.3 12.4 copy-start.1
  1320.7 89.9 %all-gather.11.cloned.1.call-start = ((), (), s32[]{:S(2)}) async-start(), calls=%async_computation.10 | async-start | bytes 1179648 | tf_op jit(solution)/shard_map/all_gather | solution.py:74
  1351.4 271.7 %all-gather.9.cloned.1.call-start = ((), (), s32[]{:S(2)}) async-start(), calls=%async_computation.6 | async-start | bytes 18874368 | tf_op jit(solution)/shard_map/all_gather | solution.py:66
  1352.2 317.2 %reduce-scatter.6.cloned.1.call-start = ((), (), s32[]{:S(2)}) async-start(), calls=%async_computation.7 | async-start | bytes 50331648 | tf_op jit(solution)/shard_map/reduce_scatter | solution.py:49
  1380.2 338.5 %reduce-scatter.8.cloned.1.call-start = ((), (), s32[]{:S(2)}) async-start(), calls=%async_computation.8 | async-start | bytes 50331648 | tf_op jit(solution)/shard_map/reduce_scatter | solution.py:50
Sparse Core Ops, SparseCore 0:
  10.1 230.2 all-gather.6
  242.6 225.7 all-gather.4
  517.1 196.6 all-reduce.5
  745.5 543.7 reduce-scatter.3
  1320.8 30.5 all-reduce.3
  1353.6 40.1 all-gather.10
  1396.7 226.3 all-gather.8
  1626.1 43.2 reduce-scatter.5
  1672.4 46.3 reduce-scatter.7
where the time goes:
time: 1740 us; the launch traced here: 1730 us
  waiting for transfers between devices  1400 us (80%)
  matrix products  213 us (12%)
  local copies, waits for them, and re-layouts  84.8 us (5%)
  other arithmetic  18.7 us (1%)
    reduce_scatter x1, waiting for transfers between devices, on_device(): lax.psum_scatter(jnp.einsum('rh,ch->rc', pre_grad, w_in, preferred_elemen...  540 us
    all_gather x1, waiting for transfers between devices, on_device(): lax.all_gather(contexts, 'tm', axis=0, tiled=True)  232 us
    all_gather x1, waiting for transfers between devices, on_device(): all_gate = lax.all_gather(own_gate, 'tm', axis=0, tiled=True)  212 us
    psum x1, waiting for transfers between devices, on_device(): hidden_pre, hidden_grad = lax.psum((hidden_part, hgrad_part), 'chan')  197 us
    all_gather x1, waiting for transfers between devices, on_device(): lax.all_gather(cotangent, 'tm', axis=0, tiled=True)  100 us
    dot_general x1, matrix products, on_device(): pre_time = jnp.dot(time_weight, flat_x, preferred_element_type=jnp.float32)  60.1 us
    reduce_scatter x1, waiting for transfers between devices, on_device(): lax.psum_scatter(wout_part, 'dp', scatter_dimension=0, tiled=True)  49.4 us
  transfers between devices with their start and end apart: 9, of which 8 were waited for; matrix products, arithmetic and copies ran while one was open for 12% of the time, Pallas kernels for 0%

commit v1 on v0

v1 whole, which is shorter than its diff:
```python
import math

import jax
import jax.numpy as jnp
from jax import lax
from jax.sharding import PartitionSpec as P

tanh_scale = math.sqrt(2.0 / math.pi)
cubic_term = 0.044715


def gelu_pair(value):
    inner = jnp.tanh(tanh_scale * (value + cubic_term * value * value * value))
    result = 0.5 * value * (1.0 + inner)
    slope = 0.5 * (1.0 + inner) + 0.5 * value * (1.0 - inner * inner) * tanh_scale * (
        1.0 + 3.0 * cubic_term * value * value
    )
    return (result, slope)


def hidden_finish(hidden_pre, hidden_grad):
    act_hidden, slope_hidden = gelu_pair(hidden_pre)
    return (act_hidden.astype(jnp.bfloat16), (hidden_grad * slope_hidden).astype(jnp.bfloat16))


def dot(lhs, rhs, lhs_dim, rhs_dim):
    return lax.dot_general(
        lhs, rhs, (((lhs_dim,), (rhs_dim,)), ((), ())), preferred_element_type=jnp.float32
    )


def shifted(value, axis, count, step):
    return lax.ppermute(value, axis, [(i, (i + step) % count) for i in range(count)])


def body(chan_count, tm_count, dp_count):
    def chan_sum(part):
        total = part
        narrow = part.astype(jnp.bfloat16)
        for step in range(1, chan_count):
            total = total + shifted(narrow, "chan", chan_count, step).astype(jnp.float32)
        return total

    def dp_scatter(product, split):
        here = lax.axis_index("dp")
        arrived = []
        for step in range(1, dp_count):
            there = (here + step) % dp_count
            term = product(lax.dynamic_slice_in_dim(split, there * (split.shape[1] // dp_count), split.shape[1] // dp_count, 1))
            arrived.append(shifted(term.astype(jnp.bfloat16), "dp", dp_count, step))
        size = split.shape[1] // dp_count
        total = product(lax.dynamic_slice_in_dim(split, here * size, size, 1))
        for term in arrived:
            total = total + term.astype(jnp.float32)
        return total

    def on_device(contexts, cotangent, w_in, w_out, time_weight):
        local_len, windows, width = contexts.shape
        own_width = width // tm_count
        position = lax.axis_index("tm")

        def own(array):
            return lax.dynamic_slice_in_dim(array, position * own_width, own_width, 1)

        xs, dys, mixeds, acts, grads, feats = [], [], [], [], [], []
        for b in range(windows):
            x = lax.all_gather(contexts[:, b, :], "tm", axis=0, tiled=True)
            dy = lax.all_gather(cotangent[:, b, :], "tm", axis=0, tiled=True)
            xs.append(x)
            dys.append(dy)
        for b in range(windows):
            x, dy = xs[b], dys[b]
            act_time, _ = gelu_pair(dot(time_weight, x, 1, 0))
            mixed = (x.astype(jnp.float32) + act_time).astype(jnp.bfloat16)
            hidden_pre = chan_sum(dot(mixed, w_in, 1, 0))
            hidden_grad = chan_sum(dot(dy, w_out, 1, 1))
            activation, pre_grad = hidden_finish(hidden_pre, hidden_grad)
            mixeds.append(mixed)
            acts.append(activation)
            grads.append(pre_grad)
            feature = dot(pre_grad, w_in, 1, 1).astype(jnp.bfloat16)
            feats.append(lax.psum_scatter(feature, "tm", scatter_dimension=1, tiled=True))

        outs = []
        time_part = None
        for b in range(windows):
            x_own, dy_own = own(xs[b]), own(dys[b])
            _, slope = gelu_pair(dot(time_weight, x_own, 1, 0))
            mixed_grad = dy_own.astype(jnp.float32) + feats[b].astype(jnp.float32)
            gate = (mixed_grad * slope).astype(jnp.bfloat16)
            back = dot(time_weight, gate, 0, 0)
            outs.append(
                lax.all_to_all(
                    (mixed_grad + back).astype(jnp.bfloat16), "tm", 0, 1, tiled=True
                )
            )
            term = dot(gate, x_own, 1, 1)
            time_part = term if time_part is None else time_part + term
        grad_time = lax.psum(time_part, ("chan", "tm", "dp"))
        grad_contexts = jnp.stack(outs, axis=1)

        mixed_rows = jnp.concatenate(mixeds, axis=0)
        dy_rows = jnp.concatenate(dys, axis=0)
        grad_w_in = dp_scatter(
            lambda part: dot(mixed_rows, part, 0, 0), jnp.concatenate(grads, axis=0)
        )
        grad_w_out = dp_scatter(
            lambda part: dot(part, dy_rows, 0, 0), jnp.concatenate(acts, axis=0)
        )
        return (grad_contexts, grad_w_in, grad_w_out, grad_time)

    return on_device


def solution(mesh):
    return jax.shard_map(
        body(mesh.shape["chan"], mesh.shape["tm"], mesh.shape["dp"]),
        mesh=mesh,
        in_specs=(
            P("tm", "dp", "chan"),
            P("tm", "dp", "chan"),
            P("chan", "tm"),
            P("tm", "chan"),
            P(),
        ),
        out_specs=(P("tm", "dp", "chan"), P("chan", ("tm", "dp")), P(("tm", "dp"), "chan"), P()),
        check_vma=False,
    )
```

time: 1740 us -> 1030 us (0.59)
  waiting for transfers between devices: 1400 us -> 714 us
  local copies, waits for them, and re-layouts: 84.8 us -> 36.5 us
  matrix products: 213 us -> 235 us
    reduce_scatter x3 -> x2, waiting for transfers between devices: 622 us -> 178 us  [on_device(): lax.psum_scatter(feature, 'tm', scatter_dimension=1, tiled=True)]
    all_gather x4, waiting for transfers between devices: 544 us -> 369 us  [the longest x2 217 us: on_device(): x = lax.all_gather(contexts[:, b, :], 'tm', axis=0, tiled=True)]
    psum x2 -> x1, waiting for transfers between devices: 227 us -> 121 us  [on_device(): grad_time = lax.psum(time_part, ('chan', 'tm', 'dp'))]
    reshape x3 -> x0, local copies, waits for them, and re-layouts: 55.5 us -> none  [the longest x1 25.5 us: on_device(): mixed = (flat_x.astype(jnp.float32) + act_time).astype(jnp.bfloat16).resh...]
    ppermute x0 -> x6, waiting for transfers between devices: none -> 46.1 us  [shifted(): lax.ppermute(value, axis, [(i, (i + step) % count) for i in range(count)])]
    dot_general x8 -> x18, matrix products: 213 us -> 235 us  [dot(): lax.dot_general(lhs, rhs, (((lhs_dim,), (rhs_dim,)), ((), ())), preferred...]
  transfers between devices with their start and end apart: 9 -> 15, of which waited for: 8 -> 9; matrix products, arithmetic and copies ran while one was open for 12% -> 26% of each run, Pallas kernels for 0% -> 0%
where the time goes in v1:
time: 1030 us; the launch traced here: 1020 us
  waiting for transfers between devices  714 us (69%)
  matrix products  235 us (23%)
  local copies, waits for them, and re-layouts  36.5 us (4%)
  between operations  14.8 us (1%)
  starting transfers between devices  14.5 us (1%)
    dot_general x18, matrix products, dot(): lax.dot_general(lhs, rhs, (((lhs_dim,), (rhs_dim,)), ((), ())), preferred...  235 us
    all_gather x2, waiting for transfers between devices, on_device(): x = lax.all_gather(contexts[:, b, :], 'tm', axis=0, tiled=True)  217 us
    reduce_scatter x2, waiting for transfers between devices, on_device(): lax.psum_scatter(feature, 'tm', scatter_dimension=1, tiled=True)  178 us
    all_gather x2, waiting for transfers between devices, on_device(): dy = lax.all_gather(cotangent[:, b, :], 'tm', axis=0, tiled=True)  152 us
    psum x1, waiting for transfers between devices, on_device(): grad_time = lax.psum(time_part, ('chan', 'tm', 'dp'))  121 us
    ppermute x6, waiting for transfers between devices, shifted(): lax.ppermute(value, axis, [(i, (i + step) % count) for i in range(count)])  46.1 us
  transfers between devices with their start and end apart: 15, of which 9 were waited for; matrix products, arithmetic and copies ran while one was open for 26% of the time, Pallas kernels for 0%

profile of v1, /device:TPU:0, one launch (start us, length us, event | category | flops | bytes accessed | tf_op | source)
XLA Modules:
  0.0 1023.9 jit_solution(16191625148046705877)
XLA Ops:
  7.2 6.9 fusion.90
  14.1 2.1 copy.37
  16.3 3.8 fusion.89
  20.2 2.1 copy.38
  22.4 2.1 copy.39
  24.5 3.7 copy.40
  28.6 115.5 %all-gather.9.cloned.1.call-done = bf16[512,1,8192]{2,0,1:T(8,128)(2,1)} async-done(((bf16[64,1,8192]{2,0,1:T(8,128)(2,1)}), bf16[512,1,8192]{2,0,1:T(8,128)(2,1)}) %all-gather.9.cloned.1.call-update) | async-done | bytes 8388624 | tf_op jit(solution)/shard_map/all_gather | solution.py:68
  144.1 15.6 %fusion.94 = (bf16[512,1024]{1,0:T(8,128)(2,1)}, f32[512,1024]{1,0:T(8,128)S(1)}) fusion(bf16[1024,8192]{1,0:T(8,128)(2,1)} %param.8, bf16[512,1,8192]{2,0,1:T(8,128)(2,1)} %all-gather.9.cloned.1.call-done), kind=kOutput, calls=%fused_computation.124 | convolution fusion | flops 8590458880 | bytes 28311552 | tf_op jit(solution)/shard_map/dot_general | solution.py:27
  159.7 1.5 collective-permute-start
  161.2 108.2 %all-gather.11.cloned.1.call-done = bf16[512,1,8192]{2,0,1:T(8,128)(2,1)} async-done(((bf16[64,1,8192]{2,0,1:T(8,128)(2,1)}), bf16[512,1,8192]{2,0,1:T(8,128)(2,1)}) %all-gather.11.cloned.1.call-update) | async-done | bytes 8388624 | tf_op jit(solution)/shard_map/all_gather | solution.py:67
  269.3 14.3 %fusion.5 = bf16[512,8192]{1,0:T(8,128)(2,1)S(1)} fusion(bf16[512,1,8192]{2,0,1:T(8,128)(2,1)} %all-gather.11.cloned.1.call-done, bf16[512,512]{1,0:T(8,128)(2,1)S(1)} %copy-done), kind=kOutput, calls=%fused_computation.7 | convolution fusion | flops 4341104640 | bytes 17301504 | tf_op jit(solution)/shard_map/dot_general | solution.py:27
  283.6 15.2 %fusion.93 = (bf16[512,1024]{1,0:T(8,128)(2,1)S(1)}, f32[512,1024]{1,0:T(8,128)S(1)}) fusion(bf16[512,8192]{1,0:T(8,128)(2,1)S(1)} %fusion.5, bf16[8192,1024]{1,0:T(8,128)(2,1)} %param.7), kind=kOutput, calls=%fused_computation.123 | convolution fusion | flops 8590458880 | bytes 28311552 | tf_op jit(solution)/shard_map/dot_general | solution.py:27
  298.8 1.5 collective-permute-start.1
  300.4 23.0 %collective-permute-done.1 = bf16[512,1024]{1,0:T(8,128)(2,1)S(1)} collective-permute-done((bf16[512,1024]{1,0:T(8,128)(2,1)S(1)}, bf16[512,1024]{1,0:T(8,128)(2,1)S(1)}, u32[]{:S(2)}, u32[]{:S(2)}) %collective-permute-start.1) | collective-permute-done | bytes 1048608 | tf_op jit(solution)/shard_map/ppermute | solution.py:33
  323.4 4.0 multiply_convert_fusion.1
  328.4 30.2 %convolution_convert_fusion.3 = bf16[512,8192]{1,0:T(8,128)(2,1)} fusion(bf16[512,1024]{1,0:T(8,128)(2,1)S(1)} %get-tuple-element.15, bf16[8192,1024]{1,0:T(8,128)(2,1)} %param.7), kind=kOutput, calls=%fused_computation.21 | convolution fusion | flops 8594128896 | bytes 26214400 | tf_op jit(solution)/shard_map/dot_general | solution.py:27
  358.7 36.5 %all-gather.13.cloned.1.call-done = bf16[512,1,8192]{2,0,1:T(8,128)(2,1)} async-done(((bf16[64,1,8192]{2,0,1:T(8,128)(2,1)}), bf16[512,1,8192]{2,0,1:T(8,128)(2,1)}) %all-gather.13.cloned.1.call-update) | async-done | bytes 8388624 | tf_op jit(solution)/shard_map/all_gather | solution.py:68
  395.2 15.6 %fusion.92 = (bf16[512,1024]{1,0:T(8,128)(2,1)}, f32[512,1024]{1,0:T(8,128)S(1)}) fusion(bf16[1024,8192]{1,0:T(8,128)(2,1)} %param.8, bf16[512,1,8192]{2,0,1:T(8,128)(2,1)} %all-gather.13.cloned.1.call-done), kind=kOutput, calls=%fused_computation.122 | convolution fusion | flops 8590458880 | bytes 28311552 | tf_op jit(solution)/shard_map/dot_general | solution.py:27
  410.8 1.5 collective-permute-start.2
  412.3 108.6 %all-gather.15.cloned.1.call-done = bf16[512,1,8192]{2,0,1:T(8,128)(2,1)} async-done(((bf16[64,1,8192]{2,0,1:T(8,128)(2,1)}), bf16[512,1,8192]{2,0,1:T(8,128)(2,1)}) %all-gather.15.cloned.1.call-update) | async-done | bytes 8388624 | tf_op jit(solution)/shard_map/all_gather | solution.py:67
  520.9 14.3 %fusion.11 = bf16[512,8192]{1,0:T(8,128)(2,1)S(1)} fusion(bf16[512,1,8192]{2,0,1:T(8,128)(2,1)} %all-gather.15.cloned.1.call-done, bf16[512,512]{1,0:T(8,128)(2,1)S(1)} %copy-done), kind=kOutput, calls=%fused_computation.13 | convolution fusion | flops 4341104640 | bytes 17301504 | tf_op jit(solution)/shard_map/dot_general | solution.py:27
  535.2 15.2 %fusion.91 = (bf16[512,1024]{1,0:T(8,128)(2,1)S(1)}, f32[512,1024]{1,0:T(8,128)S(1)}) fusion(bf16[512,8192]{1,0:T(8,128)(2,1)S(1)} %fusion.11, bf16[8192,1024]{1,0:T(8,128)(2,1)} %param.7), kind=kOutput, calls=%fused_computation.121 | convolution fusion | flops 8590458880 | bytes 28311552 | tf_op jit(solution)/shard_map/dot_general | solution.py:27
  550.4 1.5 collective-permute-start.3
  552.0 23.0 %collective-permute-done.3 = bf16[512,1024]{1,0:T(8,128)(2,1)S(1)} collective-permute-done((bf16[512,1024]{1,0:T(8,128)(2,1)S(1)}, bf16[512,1024]{1,0:T(8,128)(2,1)S(1)}, u32[]{:S(2)}, u32[]{:S(2)}) %collective-permute-start.3) | collective-permute-done | bytes 1048608 | tf_op jit(solution)/shard_map/ppermute | solution.py:33
  575.0 3.9 multiply_convert_fusion
  579.9 30.0 %convolution_convert_fusion.2 = bf16[512,8192]{1,0:T(8,128)(2,1)} fusion(bf16[512,1024]{1,0:T(8,128)(2,1)S(1)} %get-tuple-element.13, bf16[8192,1024]{1,0:T(8,128)(2,1)} %param.7), kind=kOutput, calls=%fused_computation.20 | convolution fusion | flops 8594128896 | bytes 26214400 | tf_op jit(solution)/shard_map/dot_general | solution.py:27
  609.9 1.2 copy-done.8
  611.1 15.0 %convolution_convert_fusion = bf16[512,8192]{1,0:T(8,128)(2,1)} fusion(bf16[512,8192]{1,0:T(8,128)(2,1)} %bitcast.101, bf16[512,8192]{1,0:T(8,128)(2,1)} %bitcast.99, s32[]{:T(128)S(6)} %select_n.26, bf16[512,1024]{1,0:T(8,128)(2,1)S(1)} %copy-done.8, bf16[512,1024]{1,0:T(8,128)(2,1)} %get-tuple-element.12), kind=kOutput, calls=%fused_computation.18 | convolution fusion | flops 8629780480 | bytes 27262980 | tf_op jit(solution)/shard_map/dot_general | solution.py:27
  626.2 14.9 %convolution_convert_fusion.1 = bf16[8192,512]{1,0:T(8,128)(2,1)} fusion(bf16[512,8192]{1,0:T(8,128)(2,1)} %copy-done.14, bf16[512,8192]{1,0:T(8,128)(2,1)} %copy-done.13, s32[]{:T(128)S(6)} %select_n.26, bf16[512,1024]{1,0:T(8,128)(2,1)S(1)} %copy-done.7, bf16[512,1024]{1,0:T(8,128)(2,1)} %copy-done.9), kind=kOutput, calls=%fused_computation.19 | convolution fusion | flops 8629780480 | bytes 27262980 | tf_op jit(solution)/shard_map/dot_general | solution.py:27
  641.5 31.0 %reduce-scatter.3.cloned.1.call-done = bf16[512,1024]{1,0:T(8,128)(2,1)} async-done(((bf16[512,8192]{1,0:T(8,128)(2,1)}), bf16[512,1024]{1,0:T(8,128)(2,1)}) %reduce-scatter.3.cloned.1.call-update) | async-done | bytes 1048592 | tf_op jit(solution)/shard_map/reduce_scatter | solution.py:82
  672.5 3.9 fusion.35
  676.5 3.4 fusion.53
  679.9 3.9 all-to-all-start
  683.8 17.4 %convert_add_fusion = f32[512,8192]{1,0:T(8,128)} fusion(bf16[512,8192]{1,0:T(8,128)(2,1)} %collective-permute-done.5, bf16[512,8192]{1,0:T(8,128)(2,1)} %bitcast.102, bf16[512,8192]{1,0:T(8,128)(2,1)} %bitcast.100, s32[]{:T(128)S(6)} %select_n.24, bf16[512,1024]{1,0:T(8,128)(2,1)S(1)} %copy-done.8, bf16[512,1024]{1,0:T(8,128)(2,1)} %get-tuple-element.12), kind=kOutput, calls=%fused_computation.16 | convolution fusion | flops 8633974784 | bytes 44040196 | tf_op jit(solution)/shard_map/dot_general | solution.py:27
  701.2 147.1 %reduce-scatter.5.cloned.1.call-done = bf16[512,1024]{1,0:T(8,128)(2,1)} async-done(((bf16[512,8192]{1,0:T(8,128)(2,1)}), bf16[512,1024]{1,0:T(8,128)(2,1)}) %reduce-scatter.5.cloned.1.call-update) | async-done | bytes 1048592 | tf_op jit(solution)/shard_map/reduce_scatter | solution.py:82
  848.3 3.9 fusion.49
  853.2 3.0 fusion.50
  856.2 3.6 all-to-all-start.1
  859.9 17.7 %convert_add_fusion.1 = f32[8192,512]{1,0:T(8,128)} fusion(bf16[8192,512]{1,0:T(8,128)(2,1)} %collective-permute-done.4, bf16[512,8192]{1,0:T(8,128)(2,1)} %copy-done.14, bf16[512,8192]{1,0:T(8,128)(2,1)} %copy-done.13, s32[]{:T(128)S(6)} %select_n.24, bf16[512,1024]{1,0:T(8,128)(2,1)} %copy-done.6, bf16[512,1024]{1,0:T(8,128)(2,1)} %copy-done.9), kind=kOutput, calls=%fused_computation.17 | convolution fusion | flops 8633974784 | bytes 44040196 | tf_op jit(solution)/shard_map/dot_general | solution.py:27
  877.6 2.4 fusion.66
  880.0 3.0 convolution_add_fusion
  883.0 1.5 copy.29
  884.5 2.3 stack.9
  887.5 1.3 stack.10
  888.8 1.5 pad_maximum_fusion.10
  890.2 3.5 copy.34
  893.7 120.6 %all-reduce.2.cloned.1.call-done = f32[512,512]{1,0:T(8,128)} async-done(((f32[512,512]{1,0:T(8,128)}), f32[512,512]{1,0:T(8,128)}) %all-reduce.2.cloned.1.call-update) | async-done | bytes 1048592 | tf_op jit(solution)/shard_map/psum | solution.py:99
  1014.3 2.3 copy.42
  (52 shorter events, 4.7 us)
Async XLA Ops:
  7.2 262.2 %copy-start = (bf16[512,512]{1,0:T(8,128)(2,1)S(1)}, bf16[512,512]{1,0:T(8,128)(2,1)}, u32[]{:S(2)}) copy-start(bf16[512,512]{1,0:T(8,128)(2,1)} %param.9) | copy-start | bytes 1572868
  7.2 136.9 %all-gather.9.cloned.1.call-start = ((), (), s32[]{:S(2)}) async-start(), calls=%async_computation.7 | async-start | bytes 9437184 | tf_op jit(solution)/shard_map/all_gather | solution.py:68
  14.1 2.2 copy-start.1
  16.3 253.1 %all-gather.11.cloned.1.call-start = ((), (), s32[]{:S(2)}) async-start(), calls=%async_computation.8 | async-start | bytes 9437184 | tf_op jit(solution)/shard_map/all_gather | solution.py:67
  20.1 2.2 copy-start.2
  22.3 372.9 %all-gather.13.cloned.1.call-start = ((), (), s32[]{:S(2)}) async-start(), calls=%async_computation.9 | async-start | bytes 9437184 | tf_op jit(solution)/shard_map/all_gather | solution.py:68
  24.5 496.4 %all-gather.15.cloned.1.call-start = ((), (), s32[]{:S(2)}) async-start(), calls=%async_computation.10 | async-start | bytes 9437184 | tf_op jit(solution)/shard_map/all_gather | solution.py:67
  28.3 644.2 %reduce-scatter.3.cloned.1.call-start = ((), (), s32[]{:S(2)}) async-start(), calls=%async_computation.4 | async-start | bytes 9437184 | tf_op jit(solution)/shard_map/reduce_scatter | solution.py:82
  159.7 140.7 %collective-permute-start = (bf16[512,1024]{1,0:T(8,128)(2,1)}, bf16[512,1024]{1,0:T(8,128)(2,1)}, u32[]{:S(2)}, u32[]{:S(2)}) collective-permute-start(bf16[512,1024]{1,0:T(8,128)(2,1)} %get-tuple-element.26), channel_id=1, source_target_pairs={{0,16},{16,0},{1,17},{17,1},{2,18},{18,2},{3,19},{19,3},{4,20},{20... | collective-permute-start | bytes 3145736 | tf_op jit(solution)/shard_map/ppermute | solution.py:33
  283.6 15.2 %copy-start.13 = (bf16[512,8192]{1,0:T(8,128)(2,1)}, bf16[512,8192]{1,0:T(8,128)(2,1)S(1)}, u32[]{:S(2)}) copy-start(bf16[512,8192]{1,0:T(8,128)(2,1)S(1)} %fusion.5) | copy-start | bytes 25165828
  298.8 24.6 %collective-permute-start.1 = (bf16[512,1024]{1,0:T(8,128)(2,1)S(1)}, bf16[512,1024]{1,0:T(8,128)(2,1)S(1)}, u32[]{:S(2)}, u32[]{:S(2)}) collective-permute-start(bf16[512,1024]{1,0:T(8,128)(2,1)S(1)} %get-tuple-element.24), channel_id=1, source_target_pairs={{0,16},{16,0},{1,17},{17,1},{2,18},{18,2},{3,19},{19,3},{4,20},{20... | collective-permute-start | bytes 3145736 | tf_op jit(solution)/shard_map/ppermute | solution.py:33
  327.4 1.0 copy-start.6
  358.6 489.7 %reduce-scatter.5.cloned.1.call-start = ((), (), s32[]{:S(2)}) async-start(), calls=%async_computation.5 | async-start | bytes 9437184 | tf_op jit(solution)/shard_map/reduce_scatter | solution.py:82
  410.8 141.2 %collective-permute-start.2 = (bf16[512,1024]{1,0:T(8,128)(2,1)}, bf16[512,1024]{1,0:T(8,128)(2,1)}, u32[]{:S(2)}, u32[]{:S(2)}) collective-permute-start(bf16[512,1024]{1,0:T(8,128)(2,1)} %get-tuple-element.22), channel_id=1, source_target_pairs={{0,16},{16,0},{1,17},{17,1},{2,18},{18,2},{3,19},{19,3},{4,20},{20... | collective-permute-start | bytes 3145736 | tf_op jit(solution)/shard_map/ppermute | solution.py:33
  535.2 15.2 %copy-start.14 = (bf16[512,8192]{1,0:T(8,128)(2,1)}, bf16[512,8192]{1,0:T(8,128)(2,1)S(1)}, u32[]{:S(2)}) copy-start(bf16[512,8192]{1,0:T(8,128)(2,1)S(1)} %fusion.11) | copy-start | bytes 25165828
  550.4 24.6 %collective-permute-start.3 = (bf16[512,1024]{1,0:T(8,128)(2,1)S(1)}, bf16[512,1024]{1,0:T(8,128)(2,1)S(1)}, u32[]{:S(2)}, u32[]{:S(2)}) collective-permute-start(bf16[512,1024]{1,0:T(8,128)(2,1)S(1)} %get-tuple-element.20), channel_id=1, source_target_pairs={{0,16},{16,0},{1,17},{17,1},{2,18},{18,2},{3,19},{19,3},{4,20},{20... | collective-permute-start | bytes 3145736 | tf_op jit(solution)/shard_map/ppermute | solution.py:33
  578.9 1.0 copy-start.9
  609.9 1.2 copy-start.8
  611.1 15.0 %copy-start.7 = (bf16[512,1024]{1,0:T(8,128)(2,1)S(1)}, bf16[512,1024]{1,0:T(8,128)(2,1)}, u32[]{:S(2)}) copy-start(bf16[512,1024]{1,0:T(8,128)(2,1)} %copy-done.6) | copy-start | bytes 3145732
  626.2 57.6 %collective-permute-start.5 = (bf16[512,8192]{1,0:T(8,128)(2,1)}, bf16[512,8192]{1,0:T(8,128)(2,1)}, u32[]{:S(2)}, u32[]{:S(2)}) collective-permute-start(bf16[512,8192]{1,0:T(8,128)(2,1)} %convolution_convert_fusion), channel_id=1, source_target_pairs={{0,1},{1,0},{2,3},{3,2},{4,5},{5,4},{6,7},{7,6},{8,9},{9,8},{10,11... | collective-permute-start | bytes 25165832 | tf_op jit(solution)/shard_map/ppermute | solution.py:33
  641.0 218.8 %collective-permute-start.4 = (bf16[8192,512]{1,0:T(8,128)(2,1)}, bf16[8192,512]{1,0:T(8,128)(2,1)}, u32[]{:S(2)}, u32[]{:S(2)}) collective-permute-start(bf16[8192,512]{1,0:T(8,128)(2,1)} %convolution_convert_fusion.1), channel_id=1, source_target_pairs={{0,1},{1,0},{2,3},{3,2},{4,5},{5,4},{6,7},{7,6},{8,9},{9,8},{10,11... | collective-permute-start | bytes 25165832 | tf_op jit(solution)/shard_map/ppermute | solution.py:33
  672.5 3.9 copy-start.10
  676.5 3.4 copy-start.12
  679.9 176.4 %all-to-all-start = ((bf16[8,64,1024]{2,1,0:T(8,128)(2,1)}), bf16[8,64,1024]{2,1,0:T(8,128)(2,1)S(1)}, u32[]{:S(2)}, u32[]{:S(2)}) async-start(bf16[8,64,1024]{2,1,0:T(8,128)(2,1)} %bitcast.6), calls=%async_computation.1 | async-start | bytes 2097152 | tf_op jit(solution)/shard_map/all_to_all | solution.py:93
  848.3 4.9 copy-start.11
  852.2 1.0 copy-start.4
  856.2 30.6 %all-to-all-start.1 = ((bf16[8,64,1024]{2,1,0:T(8,128)(2,1)}), bf16[8,64,1024]{2,1,0:T(8,128)(2,1)S(1)}, u32[]{:S(2)}, u32[]{:S(2)}) async-start(bf16[8,64,1024]{2,1,0:T(8,128)(2,1)} %bitcast.98), calls=%async_computation.3 | async-start | bytes 2097152 | tf_op jit(solution)/shard_map/all_to_all | solution.py:93
  859.8 154.5 %all-reduce.2.cloned.1.call-start = ((), (), s32[]{:S(2)}) async-start(), calls=%async_computation.6 | async-start | bytes 2097152 | tf_op jit(solution)/shard_map/psum | solution.py:99
  877.6 2.4 copy-start.5
  887.4 1.3 copy-start.3
Sparse Core Ops, SparseCore 0:
  16.4 127.6 all-gather.8
  146.2 123.1 all-gather.10
  272.0 123.1 all-gather.12
  397.7 123.1 all-gather.14
  524.9 147.5 reduce-scatter.2
  677.0 171.2 reduce-scatter.4
  883.1 131.1 all-reduce.1

commit v2 on v1

--- a/solution.py
+++ b/solution.py
@@ -54,6 +54,47 @@
             total = total + term.astype(jnp.float32)
         return total
 
+    outer = min(4, tm_count)
+    inner = tm_count // outer
+
+    def line_gather(block):
+        rows = block.shape[0]
+        position = lax.axis_index("tm")
+        far, near = position // inner, position % inner
+        up = [(i, i + inner) for i in range(tm_count - inner)]
+        down = [(i + inner, i) for i in range(tm_count - inner)]
+        lower, upper = [block], [block]
+        for _ in range(1, outer):
+            lower.append(lax.ppermute(lower[-1], "tm", up))
+            upper.append(lax.ppermute(upper[-1], "tm", down))
+        whole = jnp.zeros((rows * tm_count, block.shape[1]), block.dtype)
+        for k in range(outer):
+            piece = block if k == 0 else jnp.where(far + k < outer, upper[k], lower[outer - k])
+            line = (far + k) % outer
+            for step in range(inner):
+                if step == 0:
+                    landed = piece
+                else:
+                    pairs = [
+                        (i, i // inner * inner + (i % inner + step) % inner)
+                        for i in range(tm_count)
+                    ]
+                    landed = lax.ppermute(piece, "tm", pairs)
+                owner = line * inner + (near + inner - step) % inner
+                whole = lax.dynamic_update_slice(whole, landed, (owner * rows, 0))
+        return whole
+
+    def full_sum(part):
+        rows = part.shape[0] // tm_count
+        terms = lax.all_to_all(part, "tm", 0, 0, tiled=True)
+        total = terms.reshape(tm_count, rows, part.shape[1]).sum(axis=0)
+        for axis, count in (("chan", chan_count), ("dp", dp_count)):
+            if count == 2:
+                total = total + shifted(total, axis, count, 1)
+            else:
+                total = lax.psum(total, axis)
+        return lax.all_to_all(jnp.tile(total, (tm_count, 1)), "tm", 0, 0, tiled=True)
+
     def on_device(contexts, cotangent, w_in, w_out, time_weight):
         local_len, windows, width = contexts.shape
         own_width = width // tm_count
@@ -64,11 +105,16 @@
 
         xs, dys, mixeds, acts, grads, feats = [], [], [], [], [], []
         for b in range(windows):
-            x = lax.all_gather(contexts[:, b, :], "tm", axis=0, tiled=True)
             dy = lax.all_gather(cotangent[:, b, :], "tm", axis=0, tiled=True)
+            block = contexts[:, b, :]
+            if b > 0:
+                block, xs[-1] = lax.optimization_barrier((block, xs[-1]))
+            x = line_gather(block)
             xs.append(x)
             dys.append(dy)
         for b in range(windows):
+            if b > 0:
+                xs[b], dys[b], grads[-1] = lax.optimization_barrier((xs[b], dys[b], grads[-1]))
             x, dy = xs[b], dys[b]
             act_time, _ = gelu_pair(dot(time_weight, x, 1, 0))
             mixed = (x.astype(jnp.float32) + act_time).astype(jnp.bfloat16)
@@ -96,7 +142,7 @@
             )
             term = dot(gate, x_own, 1, 1)
             time_part = term if time_part is None else time_part + term
-        grad_time = lax.psum(time_part, ("chan", "tm", "dp"))
+        grad_time = full_sum(time_part)
         grad_contexts = jnp.stack(outs, axis=1)
 
         mixed_rows = jnp.concatenate(mixeds, axis=0)

time: 1030 us -> 973 us (0.945)
  waiting for transfers between devices: 714 us -> 551 us
  starting transfers between devices: 14.5 us -> 79.5 us
  local copies, waits for them, and re-layouts: 36.5 us -> 63.8 us
  other arithmetic: 9.36 us -> 23.4 us
    ppermute x0 -> x20, waiting for transfers between devices: none -> 326 us  [the longest x6 136 us: line_gather(): lower.append(lax.ppermute(lower[-1], 'tm', up))]
    all_gather x2 -> x0, waiting for transfers between devices: 217 us -> none  [on_device(): x = lax.all_gather(contexts[:, b, :], 'tm', axis=0, tiled=True)]
    all_gather x2, waiting for transfers between devices: 152 us -> 0.01 us  [on_device(): dy = lax.all_gather(cotangent[:, b, :], 'tm', axis=0, tiled=True)]
    psum x1 -> x0, waiting for transfers between devices: 121 us -> none  [on_device(): grad_time = lax.psum(time_part, ('chan', 'tm', 'dp'))]
    ppermute x0 -> x20, starting transfers between devices: none -> 56.7 us  [the longest x6 37.1 us: line_gather(): lower.append(lax.ppermute(lower[-1], 'tm', up))]
    reduce_scatter x2, waiting for transfers between devices: 178 us -> 147 us  [on_device(): lax.psum_scatter(feature, 'tm', scatter_dimension=1, tiled=True)]
    all_to_all x2, waiting for transfers between devices: 0.01 us -> 28.8 us  [on_device(): lax.all_to_all((mixed_grad + back).astype(jnp.bfloat16), 'tm', 0, 1, tile...]
    all_to_all x0 -> x2, waiting for transfers between devices: none -> 22.5 us  [the longest x1 22.5 us: full_sum(): terms = lax.all_to_all(part, 'tm', 0, 0, tiled=True)]
  transfers between devices with their start and end apart: 15 -> 36, of which waited for: 9 -> 24; matrix products, arithmetic and copies ran while one was open for 26% -> 31% of each run, Pallas kernels for 0% -> 0%
where the time goes in v2:
time: 973 us; the launch traced here: 964 us
  waiting for transfers between devices  551 us (57%)
  matrix products  231 us (24%)
  starting transfers between devices  79.5 us (8%)
  local copies, waits for them, and re-layouts  63.8 us (7%)
  other arithmetic  23.4 us (2%)
  between operations  14.5 us (1%)
    dot_general x18, matrix products, dot(): lax.dot_general(lhs, rhs, (((lhs_dim,), (rhs_dim,)), ((), ())), preferred...  231 us
    reduce_scatter x2, waiting for transfers between devices, on_device(): lax.psum_scatter(feature, 'tm', scatter_dimension=1, tiled=True)  147 us
    ppermute x6, waiting for transfers between devices, line_gather(): lower.append(lax.ppermute(lower[-1], 'tm', up))  136 us
    ppermute x8, waiting for transfers between devices, line_gather(): landed = lax.ppermute(piece, 'tm', pairs)  113 us
    ppermute x6, waiting for transfers between devices, line_gather(): upper.append(lax.ppermute(upper[-1], 'tm', down))  76.6 us
    ppermute x6, starting transfers between devices, line_gather(): lower.append(lax.ppermute(lower[-1], 'tm', up))  37.1 us
    all_to_all x2, waiting for transfers between devices, on_device(): lax.all_to_all((mixed_grad + back).astype(jnp.bfloat16), 'tm', 0, 1, tile...  28.8 us
    ppermute x8, waiting for transfers between devices, shifted(): lax.ppermute(value, axis, [(i, (i + step) % count) for i in range(count)])  27.1 us
  transfers between devices with their start and end apart: 36, of which 24 were waited for; matrix products, arithmetic and copies ran while one was open for 31% of the time, Pallas kernels for 0%

profile of v2, /device:TPU:0, one launch (start us, length us, event | category | flops | bytes accessed | tf_op | source)
XLA Modules:
  0.0 963.9 jit_solution(17006547996108787306)
XLA Ops:
  7.3 8.5 fusion.76
  15.8 4.4 broadcast.42.clone
  22.3 5.9 collective-permute-start.3
  28.3 21.4 %collective-permute-done.3 = bf16[64,8192]{1,0:T(8,128)(2,1)} collective-permute-done((bf16[64,8192]{1,0:T(8,128)(2,1)S(1)}, bf16[64,8192]{1,0:T(8,128)(2,1)}, u32[]{:S(2)}, u32[]{:S(2)}) %collective-permute-start.3) | collective-permute-done | bytes 1048608 | tf_op jit(solution)/shard_map/ppermute | solution.py:68
  49.7 5.5 collective-permute-start.4
  55.2 3.8 fusion.75
  64.0 19.9 %collective-permute-done.4 = bf16[64,8192]{1,0:T(8,128)(2,1)} collective-permute-done((bf16[64,8192]{1,0:T(8,128)(2,1)}, bf16[64,8192]{1,0:T(8,128)(2,1)}, u32[]{:S(2)}, u32[]{:S(2)}) %collective-permute-start.4) | collective-permute-done | bytes 1048608 | tf_op jit(solution)/shard_map/ppermute | solution.py:68
  84.0 11.7 %collective-permute-start.5 = (bf16[64,8192]{1,0:T(8,128)(2,1)}, bf16[64,8192]{1,0:T(8,128)(2,1)}, u32[]{:S(2)}, u32[]{:S(2)}) collective-permute-start(bf16[64,8192]{1,0:T(8,128)(2,1)} %collective-permute-done.4), channel_id=1, source_target_pairs={{0,4},{2,6},{4,8},{6,10},{8,12},{10,14},{1,5},{3,7},{5,9},{7,11},{... | collective-permute-start | bytes 3145736 | tf_op jit(solution)/shard_map/ppermute | solution.py:68
  97.4 24.7 %collective-permute-done.2 = bf16[64,8192]{1,0:T(8,128)(2,1)} collective-permute-done((bf16[64,8192]{1,0:T(8,128)(2,1)}, bf16[64,8192]{1,0:T(8,128)(2,1)}, u32[]{:S(2)}, u32[]{:S(2)}) %collective-permute-start.2) | collective-permute-done | bytes 1048608 | tf_op jit(solution)/shard_map/ppermute | solution.py:69
  122.1 10.1 %collective-permute-done.5 = bf16[64,8192]{1,0:T(8,128)(2,1)} collective-permute-done((bf16[64,8192]{1,0:T(8,128)(2,1)}, bf16[64,8192]{1,0:T(8,128)(2,1)}, u32[]{:S(2)}, u32[]{:S(2)}) %collective-permute-start.5) | collective-permute-done | bytes 1048608 | tf_op jit(solution)/shard_map/ppermute | solution.py:68
  138.0 38.6 %collective-permute-done.6 = bf16[64,8192]{1,0:T(8,128)(2,1)} collective-permute-done((bf16[64,8192]{1,0:T(8,128)(2,1)}, bf16[64,8192]{1,0:T(8,128)(2,1)}, u32[]{:S(2)}, u32[]{:S(2)}) %collective-permute-start.6) | collective-permute-done | bytes 1048608 | tf_op jit(solution)/shard_map/ppermute | solution.py:82
  178.9 25.0 %collective-permute-done.7 = bf16[64,8192]{1,0:T(8,128)(2,1)} collective-permute-done((bf16[64,8192]{1,0:T(8,128)(2,1)}, bf16[64,8192]{1,0:T(8,128)(2,1)}, u32[]{:S(2)}, u32[]{:S(2)}) %collective-permute-start.7) | collective-permute-done | bytes 1048608 | tf_op jit(solution)/shard_map/ppermute | solution.py:69
  209.2 21.9 %collective-permute-done.8 = bf16[64,8192]{1,0:T(8,128)(2,1)} collective-permute-done((bf16[64,8192]{1,0:T(8,128)(2,1)}, bf16[64,8192]{1,0:T(8,128)(2,1)}, u32[]{:S(2)}, u32[]{:S(2)}) %collective-permute-start.8) | collective-permute-done | bytes 1048608 | tf_op jit(solution)/shard_map/ppermute | solution.py:82
  233.4 17.7 %collective-permute-done.9 = bf16[64,8192]{1,0:T(8,128)(2,1)} collective-permute-done((bf16[64,8192]{1,0:T(8,128)(2,1)}, bf16[64,8192]{1,0:T(8,128)(2,1)}, u32[]{:S(2)}, u32[]{:S(2)}) %collective-permute-start.9) | collective-permute-done | bytes 1048608 | tf_op jit(solution)/shard_map/ppermute | solution.py:69
  257.6 21.5 %collective-permute-done.10 = bf16[64,8192]{1,0:T(8,128)(2,1)} collective-permute-done((bf16[64,8192]{1,0:T(8,128)(2,1)}, bf16[64,8192]{1,0:T(8,128)(2,1)}, u32[]{:S(2)}, u32[]{:S(2)}) %collective-permute-start.10) | collective-permute-done | bytes 1048608 | tf_op jit(solution)/shard_map/ppermute | solution.py:82
  283.9 3.7 copy.40
  290.8 27.3 %collective-permute-done.14 = bf16[64,8192]{1,0:T(8,128)(2,1)S(1)} collective-permute-done((bf16[64,8192]{1,0:T(8,128)(2,1)}, bf16[64,8192]{1,0:T(8,128)(2,1)S(1)}, u32[]{:S(2)}, u32[]{:S(2)}) %collective-permute-start.14) | collective-permute-done | bytes 1048608 | tf_op jit(solution)/shard_map/ppermute | solution.py:68
  318.1 7.0 collective-permute-start.15
  325.1 14.6 %fusion.5 = bf16[512,8192]{1,0:T(8,128)(2,1)S(1)} fusion(bf16[512,8192]{1,0:T(8,128)(2,1)} %constant_dynamic-update-slice_fusion.8, bf16[512,512]{1,0:T(8,128)(2,1)S(1)} %copy-done), kind=kOutput, calls=%fused_computation.7 | convolution fusion | flops 4341104640 | bytes 17301504 | tf_op jit(solution)/shard_map/dot_general | solution.py:27
  339.7 23.1 %collective-permute-done.15 = bf16[64,8192]{1,0:T(8,128)(2,1)S(1)} collective-permute-done((bf16[64,8192]{1,0:T(8,128)(2,1)S(1)}, bf16[64,8192]{1,0:T(8,128)(2,1)S(1)}, u32[]{:S(2)}, u32[]{:S(2)}) %collective-permute-start.15) | collective-permute-done | bytes 1048608 | tf_op jit(solution)/shard_map/ppermute | solution.py:68
  362.8 4.4 collective-permute-start.16
  367.2 4.4 broadcast.42
  375.1 33.8 %collective-permute-done.16 = bf16[64,8192]{1,0:T(8,128)(2,1)S(1)} collective-permute-done((bf16[64,8192]{1,0:T(8,128)(2,1)S(1)}, bf16[64,8192]{1,0:T(8,128)(2,1)S(1)}, u32[]{:S(2)}, u32[]{:S(2)}) %collective-permute-start.16) | collective-permute-done | bytes 1048608 | tf_op jit(solution)/shard_map/ppermute | solution.py:68
  411.9 13.4 %fusion.77 = (bf16[512,1024]{1,0:T(8,128)(2,1)}, f32[512,1024]{1,0:T(8,128)S(1)}) fusion(bf16[512,8192]{1,0:T(8,128)(2,1)S(1)} %fusion.5, bf16[8192,1024]{1,0:T(8,128)(2,1)} %param.7), kind=kOutput, calls=%fused_computation.137 | convolution fusion | flops 8590458880 | bytes 28311552 | tf_op jit(solution)/shard_map/dot_general | solution.py:27
  426.7 6.2 collective-permute-done.17
  433.9 9.2 collective-permute-done.18
  448.0 14.4 %fusion.78 = (bf16[512,1024]{1,0:T(8,128)(2,1)S(1)}, f32[512,1024]{1,0:T(8,128)S(1)}) fusion(bf16[1024,8192]{1,0:T(8,128)(2,1)} %param.8, bf16[512,1,8192]{2,0,1:T(8,128)(2,1)} %all-gather.5.cloned.1.call-done), kind=kOutput, calls=%fused_computation.138 | convolution fusion | flops 8590458880 | bytes 28311552 | tf_op jit(solution)/shard_map/dot_general | solution.py:27
  467.8 12.8 %collective-permute-done = bf16[512,1024]{1,0:T(8,128)(2,1)S(1)} collective-permute-done((bf16[512,1024]{1,0:T(8,128)(2,1)S(1)}, bf16[512,1024]{1,0:T(8,128)(2,1)S(1)}, u32[]{:S(2)}, u32[]{:S(2)}) %collective-permute-start) | collective-permute-done | bytes 1048608 | tf_op jit(solution)/shard_map/ppermute | solution.py:33
  480.6 4.0 multiply_convert_fusion.1
  485.5 29.7 %convolution_convert_fusion.3 = bf16[512,8192]{1,0:T(8,128)(2,1)} fusion(bf16[512,1024]{1,0:T(8,128)(2,1)S(1)} %get-tuple-element.13, bf16[8192,1024]{1,0:T(8,128)(2,1)} %param.7), kind=kOutput, calls=%fused_computation.23 | convolution fusion | flops 8594128896 | bytes 26214400 | tf_op jit(solution)/shard_map/dot_general | solution.py:27
  519.2 24.6 %collective-permute-done.21 = bf16[64,8192]{1,0:T(8,128)(2,1)S(1)} collective-permute-done((bf16[64,8192]{1,0:T(8,128)(2,1)S(1)}, bf16[64,8192]{1,0:T(8,128)(2,1)S(1)}, u32[]{:S(2)}, u32[]{:S(2)}) %collective-permute-start.21) | collective-permute-done | bytes 1048608 | tf_op jit(solution)/shard_map/ppermute | solution.py:82
  544.9 14.5 %fusion.80 = (bf16[512,1024]{1,0:T(8,128)(2,1)S(1)}, f32[512,1024]{1,0:T(8,128)S(1)}) fusion(bf16[512,8192]{1,0:T(8,128)(2,1)} %bitcast.97, bf16[1024,8192]{1,0:T(8,128)(2,1)} %param.8), kind=kOutput, calls=%fused_computation.140 | convolution fusion | flops 8590458880 | bytes 28311552 | tf_op jit(solution)/shard_map/dot_general | solution.py:27
  561.0 14.1 %fusion.11 = bf16[512,8192]{1,0:T(8,128)(2,1)S(1)} fusion(bf16[512,8192]{1,0:T(8,128)(2,1)} %constant_dynamic-update-slice_fusion, bf16[512,512]{1,0:T(8,128)(2,1)S(1)} %copy-done), kind=kOutput, calls=%fused_computation.13 | convolution fusion | flops 4341104640 | bytes 17301504 | tf_op jit(solution)/shard_map/dot_general | solution.py:27
  575.1 15.2 %fusion.79 = (bf16[512,1024]{1,0:T(8,128)(2,1)S(1)}, f32[512,1024]{1,0:T(8,128)S(1)}) fusion(bf16[512,8192]{1,0:T(8,128)(2,1)S(1)} %fusion.11, bf16[8192,1024]{1,0:T(8,128)(2,1)} %param.7), kind=kOutput, calls=%fused_computation.139 | convolution fusion | flops 8590458880 | bytes 28311552 | tf_op jit(solution)/shard_map/dot_general | solution.py:27
  590.9 14.2 %collective-permute-done.23 = bf16[512,1024]{1,0:T(8,128)(2,1)S(1)} collective-permute-done((bf16[512,1024]{1,0:T(8,128)(2,1)S(1)}, bf16[512,1024]{1,0:T(8,128)(2,1)S(1)}, u32[]{:S(2)}, u32[]{:S(2)}) %collective-permute-start.23) | collective-permute-done | bytes 1048608 | tf_op jit(solution)/shard_map/ppermute | solution.py:33
  608.8 30.5 %convolution_convert_fusion.2 = bf16[512,8192]{1,0:T(8,128)(2,1)} fusion(bf16[512,1024]{1,0:T(8,128)(2,1)S(1)} %get-tuple-element.37, bf16[8192,1024]{1,0:T(8,128)(2,1)} %param.7), kind=kOutput, calls=%fused_computation.22 | convolution fusion | flops 8594128896 | bytes 26214400 | tf_op jit(solution)/shard_map/dot_general | solution.py:27
  640.6 15.0 %convolution_convert_fusion = bf16[512,8192]{1,0:T(8,128)(2,1)} fusion(bf16[512,8192]{1,0:T(8,128)(2,1)} %bitcast.98, bf16[512,8192]{1,0:T(8,128)(2,1)} %bitcast.95, s32[]{:T(128)S(6)} %select_n.186, bf16[512,1024]{1,0:T(8,128)(2,1)S(1)} %copy-done.11, bf16[512,1024]{1,0:T(8,128)(2,1)} %get-tuple-element.36), kind=kOutput, calls=%fused_computation.20 | convolution fusion | flops 8629780480 | bytes 27262980 | tf_op jit(solution)/shard_map/dot_general | solution.py:27
  655.6 14.9 %convolution_convert_fusion.1 = bf16[8192,512]{1,0:T(8,128)(2,1)} fusion(bf16[512,8192]{1,0:T(8,128)(2,1)} %copy-done.15, bf16[512,8192]{1,0:T(8,128)(2,1)} %copy-done.14, s32[]{:T(128)S(6)} %select_n.186, bf16[512,1024]{1,0:T(8,128)(2,1)S(1)} %copy-done.10, bf16[512,1024]{1,0:T(8,128)(2,1)} %copy-done.12), kind=kOutput, calls=%fused_computation.21 | convolution fusion | flops 8629780480 | bytes 27262980 | tf_op jit(solution)/shard_map/dot_general | solution.py:27
  672.3 3.8 fusion.27
  679.1 146.1 %reduce-scatter.5.cloned.1.call-done = bf16[512,1024]{1,0:T(8,128)(2,1)} async-done(((bf16[512,8192]{1,0:T(8,128)(2,1)}), bf16[512,1024]{1,0:T(8,128)(2,1)}) %reduce-scatter.5.cloned.1.call-update) | async-done | bytes 1048592 | tf_op jit(solution)/shard_map/reduce_scatter | solution.py:128
  825.2 3.8 fusion.41
  840.1 22.5 %all-to-all-done.2 = f32[8,64,512]{2,1,0:T(8,128)S(1)} async-done(((f32[8,64,512]{2,1,0:T(8,128)}), f32[8,64,512]{2,1,0:T(8,128)S(1)}, u32[]{:S(2)}, u32[]{:S(2)}) %all-to-all-start.2) | async-done | bytes 1048608 | tf_op jit(solution)/shard_map/all_to_all | solution.py:89
  871.6 20.6 %all-to-all-done = bf16[8,64,1024]{2,1,0:T(8,128)(2,1)S(1)} async-done(((bf16[8,64,1024]{2,1,0:T(8,128)(2,1)}), bf16[8,64,1024]{2,1,0:T(8,128)(2,1)S(1)}, u32[]{:S(2)}, u32[]{:S(2)}) %all-to-all-start) | async-done | bytes 1048608 | tf_op jit(solution)/shard_map/all_to_all | solution.py:139
  892.2 3.9 all-to-all-start.1
  896.1 17.7 %convert_add_fusion = f32[512,8192]{1,0:T(8,128)} fusion(bf16[512,8192]{1,0:T(8,128)(2,1)} %collective-permute-done.25, bf16[512,8192]{1,0:T(8,128)(2,1)} %bitcast.101, bf16[512,8192]{1,0:T(8,128)(2,1)} %bitcast.96, s32[]{:T(128)S(6)} %select_n.184, bf16[512,1024]{1,0:T(8,128)(2,1)} %get-tuple-element.38, bf16[512,1024]{1,0:T(8,128)(2,1)} %get-tuple-element.36), kind=kOutput, calls=%fused_computation.18 | convolution fusion | flops 8633974784 | bytes 44040196 | tf_op jit(solution)/shard_map/dot_general | solution.py:27
  913.8 8.2 all-to-all-done.1
  923.1 4.3 all-to-all-start.3
  927.4 17.5 %convert_add_fusion.1 = f32[8192,512]{1,0:T(8,128)} fusion(bf16[8192,512]{1,0:T(8,128)(2,1)} %collective-permute-done.24, bf16[512,8192]{1,0:T(8,128)(2,1)} %copy-done.15, bf16[512,8192]{1,0:T(8,128)(2,1)} %copy-done.14, s32[]{:T(128)S(6)} %select_n.184, bf16[512,1024]{1,0:T(8,128)(2,1)} %copy-done.9, bf16[512,1024]{1,0:T(8,128)(2,1)} %copy-done.12), kind=kOutput, calls=%fused_computation.19 | convolution fusion | flops 8633974784 | bytes 44040196 | tf_op jit(solution)/shard_map/dot_general | solution.py:27
  (114 shorter events, 109.4 us)
Async XLA Ops:
  7.2 318.0 %copy-start = (bf16[512,512]{1,0:T(8,128)(2,1)S(1)}, bf16[512,512]{1,0:T(8,128)(2,1)}, u32[]{:S(2)}) copy-start(bf16[512,512]{1,0:T(8,128)(2,1)} %param.9) | copy-start | bytes 1572868
  7.2 440.8 %all-gather.5.cloned.1.call-start = ((), (), s32[]{:S(2)}) async-start(), calls=%async_computation.8 | async-start | bytes 9437184 | tf_op jit(solution)/shard_map/all_gather | solution.py:108
  15.8 39.3 %copy-start.1 = (bf16[64,2,8192]{2,1,0:T(2,128)(2,1)S(1)}, bf16[64,2,8192]{2,1,0:T(2,128)(2,1)}, u32[]{:S(2)}) copy-start(bf16[64,2,8192]{2,1,0:T(2,128)(2,1)} %param.6) | copy-start | bytes 6291460
  15.8 4.4 copy-start.3
  22.3 36.6 %copy-start.7 = (bf16[64,8192]{1,0:T(8,128)(2,1)}, bf16[64,8192]{1,0:T(8,128)(2,1)S(1)}, u32[]{:S(2)}) copy-start(bf16[64,8192]{1,0:T(8,128)(2,1)S(1)} %get-tuple-element.35) | copy-start | bytes 3145732
  22.3 27.4 %collective-permute-start.3 = (bf16[64,8192]{1,0:T(8,128)(2,1)S(1)}, bf16[64,8192]{1,0:T(8,128)(2,1)}, u32[]{:S(2)}, u32[]{:S(2)}) collective-permute-start(bf16[64,8192]{1,0:T(8,128)(2,1)S(1)} %get-tuple-element.35), channel_id=1, source_target_pairs={{0,4},{2,6},{4,8},{6,10},{8,12},{10,14},{1,5},{3,7},{5,9},{7,11},{... | collective-permute-start | bytes 3145736 | tf_op jit(solution)/shard_map/ppermute | solution.py:68
  49.7 34.3 %collective-permute-start.4 = (bf16[64,8192]{1,0:T(8,128)(2,1)}, bf16[64,8192]{1,0:T(8,128)(2,1)}, u32[]{:S(2)}, u32[]{:S(2)}) collective-permute-start(bf16[64,8192]{1,0:T(8,128)(2,1)} %collective-permute-done.3), channel_id=1, source_target_pairs={{0,4},{2,6},{4,8},{6,10},{8,12},{10,14},{1,5},{3,7},{5,9},{7,11},{... | collective-permute-start | bytes 3145736 | tf_op jit(solution)/shard_map/ppermute | solution.py:68
  61.1 483.8 %all-gather.7.cloned.1.call-start = ((), (), s32[]{:S(2)}) async-start(), calls=%async_computation.9 | async-start | bytes 9437184 | tf_op jit(solution)/shard_map/all_gather | solution.py:108
  61.1 35.3 %collective-permute-start.1 = (bf16[64,8192]{1,0:T(8,128)(2,1)}, bf16[64,8192]{1,0:T(8,128)(2,1)S(1)}, u32[]{:S(2)}, u32[]{:S(2)}) collective-permute-start(bf16[64,8192]{1,0:T(8,128)(2,1)} %copy-done.7), channel_id=1, source_target_pairs={{0,2},{2,0},{4,6},{6,4},{8,10},{10,8},{12,14},{14,12},{1,3},{3,1},... | collective-permute-start | bytes 3145736 | tf_op jit(solution)/shard_map/ppermute | solution.py:82
  62.7 59.4 %collective-permute-start.2 = (bf16[64,8192]{1,0:T(8,128)(2,1)}, bf16[64,8192]{1,0:T(8,128)(2,1)}, u32[]{:S(2)}, u32[]{:S(2)}) collective-permute-start(bf16[64,8192]{1,0:T(8,128)(2,1)} %copy-done.7), channel_id=1, source_target_pairs={{4,0},{6,2},{8,4},{10,6},{12,8},{14,10},{5,1},{7,3},{9,5},{11,7},{... | collective-permute-start | bytes 3145736 | tf_op jit(solution)/shard_map/ppermute | solution.py:69
  84.0 48.2 %collective-permute-start.5 = (bf16[64,8192]{1,0:T(8,128)(2,1)}, bf16[64,8192]{1,0:T(8,128)(2,1)}, u32[]{:S(2)}, u32[]{:S(2)}) collective-permute-start(bf16[64,8192]{1,0:T(8,128)(2,1)} %collective-permute-done.4), channel_id=1, source_target_pairs={{0,4},{2,6},{4,8},{6,10},{8,12},{10,14},{1,5},{3,7},{5,9},{7,11},{... | collective-permute-start | bytes 3145736 | tf_op jit(solution)/shard_map/ppermute | solution.py:68
  97.4 158.0 %copy-start.2 = (bf16[64,1,8192]{2,1,0:T(2,128)(2,1)S(1)}, bf16[64,1,8192]{2,1,0:T(2,128)(2,1)}, u32[]{:S(2)}) copy-start(bf16[64,1,8192]{2,1,0:T(2,128)(2,1)} %get-tuple-element.43) | copy-start | bytes 3145732
  135.1 41.5 %collective-permute-start.6 = (bf16[64,8192]{1,0:T(8,128)(2,1)}, bf16[64,8192]{1,0:T(8,128)(2,1)}, u32[]{:S(2)}, u32[]{:S(2)}) collective-permute-start(bf16[64,8192]{1,0:T(8,128)(2,1)} %get-tuple-element.33), channel_id=1, source_target_pairs={{0,2},{2,0},{4,6},{6,4},{8,10},{10,8},{12,14},{14,12},{1,3},{3,1},... | collective-permute-start | bytes 3145736 | tf_op jit(solution)/shard_map/ppermute | solution.py:82
  136.7 67.2 %collective-permute-start.7 = (bf16[64,8192]{1,0:T(8,128)(2,1)}, bf16[64,8192]{1,0:T(8,128)(2,1)}, u32[]{:S(2)}, u32[]{:S(2)}) collective-permute-start(bf16[64,8192]{1,0:T(8,128)(2,1)} %collective-permute-done.2), channel_id=1, source_target_pairs={{4,0},{6,2},{8,4},{10,6},{12,8},{14,10},{5,1},{7,3},{9,5},{11,7},{... | collective-permute-start | bytes 3145736 | tf_op jit(solution)/shard_map/ppermute | solution.py:69
  206.8 24.3 %collective-permute-start.8 = (bf16[64,8192]{1,0:T(8,128)(2,1)}, bf16[64,8192]{1,0:T(8,128)(2,1)}, u32[]{:S(2)}, u32[]{:S(2)}) collective-permute-start(bf16[64,8192]{1,0:T(8,128)(2,1)} %get-tuple-element.31), channel_id=1, source_target_pairs={{0,2},{2,0},{4,6},{6,4},{8,10},{10,8},{12,14},{14,12},{1,3},{3,1},... | collective-permute-start | bytes 3145736 | tf_op jit(solution)/shard_map/ppermute | solution.py:82
  207.9 43.2 %collective-permute-start.9 = (bf16[64,8192]{1,0:T(8,128)(2,1)}, bf16[64,8192]{1,0:T(8,128)(2,1)}, u32[]{:S(2)}, u32[]{:S(2)}) collective-permute-start(bf16[64,8192]{1,0:T(8,128)(2,1)} %collective-permute-done.7), channel_id=1, source_target_pairs={{4,0},{6,2},{8,4},{10,6},{12,8},{14,10},{5,1},{7,3},{9,5},{11,7},{... | collective-permute-start | bytes 3145736 | tf_op jit(solution)/shard_map/ppermute | solution.py:69
  254.0 25.1 %collective-permute-start.10 = (bf16[64,8192]{1,0:T(8,128)(2,1)}, bf16[64,8192]{1,0:T(8,128)(2,1)}, u32[]{:S(2)}, u32[]{:S(2)}) collective-permute-start(bf16[64,8192]{1,0:T(8,128)(2,1)} %get-tuple-element.29), channel_id=1, source_target_pairs={{0,2},{2,0},{4,6},{6,4},{8,10},{10,8},{12,14},{14,12},{1,3},{3,1},... | collective-permute-start | bytes 3145736 | tf_op jit(solution)/shard_map/ppermute | solution.py:82
  281.3 36.8 %collective-permute-start.14 = (bf16[64,8192]{1,0:T(8,128)(2,1)}, bf16[64,8192]{1,0:T(8,128)(2,1)S(1)}, u32[]{:S(2)}, u32[]{:S(2)}) collective-permute-start(bf16[64,8192]{1,0:T(8,128)(2,1)} %bitcast.87), channel_id=1, source_target_pairs={{0,4},{2,6},{4,8},{6,10},{8,12},{10,14},{1,5},{3,7},{5,9},{7,11},{... | collective-permute-start | bytes 3145736 | tf_op jit(solution)/shard_map/ppermute | solution.py:68
  287.6 384.6 %reduce-scatter.3.cloned.1.call-start = ((), (), s32[]{:S(2)}) async-start(), calls=%async_computation.6 | async-start | bytes 9437184 | tf_op jit(solution)/shard_map/reduce_scatter | solution.py:128
  287.7 85.0 %collective-permute-start.13 = (bf16[64,8192]{1,0:T(8,128)(2,1)}, bf16[64,8192]{1,0:T(8,128)(2,1)S(1)}, u32[]{:S(2)}, u32[]{:S(2)}) collective-permute-start(bf16[64,8192]{1,0:T(8,128)(2,1)} %bitcast.88), channel_id=1, source_target_pairs={{4,0},{6,2},{8,4},{10,6},{12,8},{14,10},{5,1},{7,3},{9,5},{11,7},{... | collective-permute-start | bytes 3145736 | tf_op jit(solution)/shard_map/ppermute | solution.py:69
  289.0 85.0 %collective-permute-start.12 = (bf16[64,8192]{1,0:T(8,128)(2,1)}, bf16[64,8192]{1,0:T(8,128)(2,1)S(1)}, u32[]{:S(2)}, u32[]{:S(2)}) collective-permute-start(bf16[64,8192]{1,0:T(8,128)(2,1)} %bitcast.89), channel_id=1, source_target_pairs={{0,2},{2,0},{4,6},{6,4},{8,10},{10,8},{12,14},{14,12},{1,3},{3,1},... | collective-permute-start | bytes 3145736 | tf_op jit(solution)/shard_map/ppermute | solution.py:82
  318.1 21.6 %copy-start.5 = (bf16[64,8192]{1,0:T(8,128)(2,1)}, bf16[64,8192]{1,0:T(8,128)(2,1)S(1)}, u32[]{:S(2)}) copy-start(bf16[64,8192]{1,0:T(8,128)(2,1)S(1)} %collective-permute-done.14) | copy-start | bytes 3145732
  318.1 44.7 %collective-permute-start.15 = (bf16[64,8192]{1,0:T(8,128)(2,1)S(1)}, bf16[64,8192]{1,0:T(8,128)(2,1)S(1)}, u32[]{:S(2)}, u32[]{:S(2)}) collective-permute-start(bf16[64,8192]{1,0:T(8,128)(2,1)S(1)} %collective-permute-done.14), channel_id=1, source_target_pairs={{0,4},{2,6},{4,8},{6,10},{8,12},{10,14},{1,5},{3,7},{5,9},{7,11},{... | collective-permute-start | bytes 3145736 | tf_op jit(solution)/shard_map/ppermute | solution.py:68
  339.7 72.2 %copy-start.14 = (bf16[512,8192]{1,0:T(8,128)(2,1)}, bf16[512,8192]{1,0:T(8,128)(2,1)S(1)}, u32[]{:S(2)}) copy-start(bf16[512,8192]{1,0:T(8,128)(2,1)S(1)} %fusion.5) | copy-start | bytes 25165828
  339.7 31.9 %copy-start.4 = (bf16[64,1,8192]{2,0,1:T(8,128)(2,1)S(1)}, bf16[64,1,8192]{2,0,1:T(8,128)(2,1)}, u32[]{:S(2)}) copy-start(bf16[64,1,8192]{2,0,1:T(8,128)(2,1)} %copy.44) | copy-start | bytes 3145732
  362.8 46.0 %collective-permute-start.16 = (bf16[64,8192]{1,0:T(8,128)(2,1)S(1)}, bf16[64,8192]{1,0:T(8,128)(2,1)S(1)}, u32[]{:S(2)}, u32[]{:S(2)}) collective-permute-start(bf16[64,8192]{1,0:T(8,128)(2,1)S(1)} %collective-permute-done.15), channel_id=1, source_target_pairs={{0,4},{2,6},{4,8},{6,10},{8,12},{10,14},{1,5},{3,7},{5,9},{7,11},{... | collective-permute-start | bytes 3145736 | tf_op jit(solution)/shard_map/ppermute | solution.py:68
  372.7 70.4 %collective-permute-start.18 = (bf16[64,8192]{1,0:T(8,128)(2,1)S(1)}, bf16[64,8192]{1,0:T(8,128)(2,1)}, u32[]{:S(2)}, u32[]{:S(2)}) collective-permute-start(bf16[64,8192]{1,0:T(8,128)(2,1)S(1)} %collective-permute-done.13), channel_id=1, source_target_pairs={{4,0},{6,2},{8,4},{10,6},{12,8},{14,10},{5,1},{7,3},{9,5},{11,7},{... | collective-permute-start | bytes 3145736 | tf_op jit(solution)/shard_map/ppermute | solution.py:69
  410.1 22.8 %collective-permute-start.17 = (bf16[64,8192]{1,0:T(8,128)(2,1)S(1)}, bf16[64,8192]{1,0:T(8,128)(2,1)S(1)}, u32[]{:S(2)}, u32[]{:S(2)}) collective-permute-start(bf16[64,8192]{1,0:T(8,128)(2,1)S(1)} %get-tuple-element.27), channel_id=1, source_target_pairs={{0,2},{2,0},{4,6},{6,4},{8,10},{10,8},{12,14},{14,12},{1,3},{3,1},... | collective-permute-start | bytes 3145736 | tf_op jit(solution)/shard_map/ppermute | solution.py:82
  425.3 42.5 %collective-permute-start.11 = (bf16[512,1024]{1,0:T(8,128)(2,1)}, bf16[512,1024]{1,0:T(8,128)(2,1)}, u32[]{:S(2)}, u32[]{:S(2)}) collective-permute-start(bf16[512,1024]{1,0:T(8,128)(2,1)} %get-tuple-element.44), channel_id=1, source_target_pairs={{0,16},{16,0},{1,17},{17,1},{2,18},{18,2},{3,19},{19,3},{4,20},{20... | collective-permute-start | bytes 3145736 | tf_op jit(solution)/shard_map/ppermute | solution.py:33
  446.0 19.5 %collective-permute-start.19 = (bf16[64,8192]{1,0:T(8,128)(2,1)}, bf16[64,8192]{1,0:T(8,128)(2,1)}, u32[]{:S(2)}, u32[]{:S(2)}) collective-permute-start(bf16[64,8192]{1,0:T(8,128)(2,1)} %get-tuple-element.25), channel_id=1, source_target_pairs={{0,2},{2,0},{4,6},{6,4},{8,10},{10,8},{12,14},{14,12},{1,3},{3,1},... | collective-permute-start | bytes 3145736 | tf_op jit(solution)/shard_map/ppermute | solution.py:82
  462.4 18.1 %collective-permute-start = (bf16[512,1024]{1,0:T(8,128)(2,1)S(1)}, bf16[512,1024]{1,0:T(8,128)(2,1)S(1)}, u32[]{:S(2)}, u32[]{:S(2)}) collective-permute-start(bf16[512,1024]{1,0:T(8,128)(2,1)S(1)} %get-tuple-element.46), channel_id=1, source_target_pairs={{0,16},{16,0},{1,17},{17,1},{2,18},{18,2},{3,19},{19,3},{4,20},{20... | collective-permute-start | bytes 3145736 | tf_op jit(solution)/shard_map/ppermute | solution.py:33
  464.0 51.3 %collective-permute-start.20 = (bf16[64,8192]{1,0:T(8,128)(2,1)}, bf16[64,8192]{1,0:T(8,128)(2,1)}, u32[]{:S(2)}, u32[]{:S(2)}) collective-permute-start(bf16[64,8192]{1,0:T(8,128)(2,1)} %collective-permute-done.18), channel_id=1, source_target_pairs={{4,0},{6,2},{8,4},{10,6},{12,8},{14,10},{5,1},{7,3},{9,5},{11,7},{... | collective-permute-start | bytes 3145736 | tf_op jit(solution)/shard_map/ppermute | solution.py:69
  515.2 1.2 copy-start.6
  515.2 310.0 %reduce-scatter.5.cloned.1.call-start = ((), (), s32[]{:S(2)}) async-start(), calls=%async_computation.7 | async-start | bytes 9437184 | tf_op jit(solution)/shard_map/reduce_scatter | solution.py:128
  518.9 24.9 %collective-permute-start.21 = (bf16[64,8192]{1,0:T(8,128)(2,1)S(1)}, bf16[64,8192]{1,0:T(8,128)(2,1)S(1)}, u32[]{:S(2)}, u32[]{:S(2)}) collective-permute-start(bf16[64,8192]{1,0:T(8,128)(2,1)S(1)} %get-tuple-element.23), channel_id=1, source_target_pairs={{0,2},{2,0},{4,6},{6,4},{8,10},{10,8},{12,14},{14,12},{1,3},{3,1},... | collective-permute-start | bytes 3145736 | tf_op jit(solution)/shard_map/ppermute | solution.py:82
  559.4 31.5 %collective-permute-start.22 = (bf16[512,1024]{1,0:T(8,128)(2,1)S(1)}, bf16[512,1024]{1,0:T(8,128)(2,1)S(1)}, u32[]{:S(2)}, u32[]{:S(2)}) collective-permute-start(bf16[512,1024]{1,0:T(8,128)(2,1)S(1)} %get-tuple-element.50), channel_id=1, source_target_pairs={{0,16},{16,0},{1,17},{17,1},{2,18},{18,2},{3,19},{19,3},{4,20},{20... | collective-permute-start | bytes 3145736 | tf_op jit(solution)/shard_map/ppermute | solution.py:33
  575.0 15.2 %copy-start.15 = (bf16[512,8192]{1,0:T(8,128)(2,1)}, bf16[512,8192]{1,0:T(8,128)(2,1)S(1)}, u32[]{:S(2)}) copy-start(bf16[512,8192]{1,0:T(8,128)(2,1)S(1)} %fusion.11) | copy-start | bytes 25165828
  590.3 14.9 %collective-permute-start.23 = (bf16[512,1024]{1,0:T(8,128)(2,1)S(1)}, bf16[512,1024]{1,0:T(8,128)(2,1)S(1)}, u32[]{:S(2)}, u32[]{:S(2)}) collective-permute-start(bf16[512,1024]{1,0:T(8,128)(2,1)S(1)} %get-tuple-element.48), channel_id=1, source_target_pairs={{0,16},{16,0},{1,17},{17,1},{2,18},{18,2},{3,19},{19,3},{4,20},{20... | collective-permute-start | bytes 3145736 | tf_op jit(solution)/shard_map/ppermute | solution.py:33
  639.4 1.2 copy-start.11
  640.6 15.0 %copy-start.10 = (bf16[512,1024]{1,0:T(8,128)(2,1)S(1)}, bf16[512,1024]{1,0:T(8,128)(2,1)}, u32[]{:S(2)}) copy-start(bf16[512,1024]{1,0:T(8,128)(2,1)} %copy-done.9) | copy-start | bytes 3145732
  655.6 240.5 %collective-permute-start.25 = (bf16[512,8192]{1,0:T(8,128)(2,1)}, bf16[512,8192]{1,0:T(8,128)(2,1)}, u32[]{:S(2)}, u32[]{:S(2)}) collective-permute-start(bf16[512,8192]{1,0:T(8,128)(2,1)} %convolution_convert_fusion), channel_id=1, source_target_pairs={{0,1},{1,0},{2,3},{3,2},{4,5},{5,4},{6,7},{7,6},{8,9},{9,8},{10,11... | collective-permute-start | bytes 25165832 | tf_op jit(solution)/shard_map/ppermute | solution.py:33
  670.5 256.9 %collective-permute-start.24 = (bf16[8192,512]{1,0:T(8,128)(2,1)}, bf16[8192,512]{1,0:T(8,128)(2,1)}, u32[]{:S(2)}, u32[]{:S(2)}) collective-permute-start(bf16[8192,512]{1,0:T(8,128)(2,1)} %convolution_convert_fusion.1), channel_id=1, source_target_pairs={{0,1},{1,0},{2,3},{3,2},{4,5},{5,4},{6,7},{7,6},{8,9},{9,8},{10,11... | collective-permute-start | bytes 25165832 | tf_op jit(solution)/shard_map/ppermute | solution.py:33
  833.0 29.6 %all-to-all-start.2 = ((f32[8,64,512]{2,1,0:T(8,128)}), f32[8,64,512]{2,1,0:T(8,128)S(1)}, u32[]{:S(2)}, u32[]{:S(2)}) async-start(f32[8,64,512]{2,1,0:T(8,128)} %bitcast.15), calls=%async_computation.4 | async-start | bytes 2097152 | tf_op jit(solution)/shard_map/all_to_all | solution.py:89
  862.6 29.6 %all-to-all-start = ((bf16[8,64,1024]{2,1,0:T(8,128)(2,1)}), bf16[8,64,1024]{2,1,0:T(8,128)(2,1)S(1)}, u32[]{:S(2)}, u32[]{:S(2)}) async-start(bf16[8,64,1024]{2,1,0:T(8,128)(2,1)} %bitcast.93), calls=%async_computation.1 | async-start | bytes 2097152 | tf_op jit(solution)/shard_map/all_to_all | solution.py:139
  866.3 5.2 collective-permute-start.26
  871.5 42.2 %collective-permute-start.27 = (f32[64,512]{1,0:T(8,128)S(1)}, f32[64,512]{1,0:T(8,128)S(1)}, u32[]{:S(2)}, u32[]{:S(2)}) collective-permute-start(f32[64,512]{1,0:T(8,128)S(1)} %add.343), channel_id=1, source_target_pairs={{0,1},{1,0},{2,3},{3,2},{4,5},{5,4},{6,7},{7,6},{8,9},{9,8},{10,11... | collective-permute-start | bytes 393224 | tf_op jit(solution)/shard_map/ppermute | solution.py:33
  892.2 29.8 %all-to-all-start.1 = ((bf16[8,64,1024]{2,1,0:T(8,128)(2,1)}), bf16[8,64,1024]{2,1,0:T(8,128)(2,1)S(1)}, u32[]{:S(2)}, u32[]{:S(2)}) async-start(bf16[8,64,1024]{2,1,0:T(8,128)(2,1)} %bitcast.94), calls=%async_computation.3 | async-start | bytes 2097152 | tf_op jit(solution)/shard_map/all_to_all | solution.py:139
  923.1 31.7 %all-to-all-start.3 = ((f32[8,64,512]{2,1,0:T(8,128)}), f32[8,64,512]{2,1,0:T(8,128)}, u32[]{:S(2)}, u32[]{:S(2)}) async-start(f32[8,64,512]{2,1,0:T(8,128)} %tile.2), calls=%async_computation.5 | async-start | bytes 2097152 | tf_op jit(solution)/shard_map/all_to_all | solution.py:96
  (4 other events, 4.0 us)
Sparse Core Ops, SparseCore 0:
  61.2 176.8 all-gather.4
  287.7 169.0 all-gather.6
  515.4 156.8 reduce-scatter.2
  676.8 148.3 reduce-scatter.4
